TPU v7x, 256 devices: a whole 4x4x8 slice. The times are simulated.
256 devices in a mesh: band: 8 (over y, z_lo), dir: 32 (over z_hi, x, core).
Axes of the slice: x: 4, y: 4, z: 8 (z_hi: 4, z_lo: 2; z = z_hi * 2 + z_lo), core: 2. Of those that a mesh axis runs over, the one named last changes fastest.
Arguments:
- responses: bfloat16 [8, 32, 2, 512, 1536], P('band', 'dir'), may hold values from -0.15625 to 0.15625
- fluxes: float32 [8, 32, 1536], P('band', 'dir'), may hold values from 0.1 to 1.5
- counts: int32 [32], P('dir'), may hold values from 512 to 1536, as said below
- penalty: float32 [32], replicated, may hold values from 0.3 to 3
- visibilities: float32 [8, 2, 512, 512], P('band', None, 'dir'), may hold values from -3 to 3
- start_gains: float32 [8, 2, 32, 512], P('band', None, None, 'dir'), may hold values from 0.5 to 1.5
Outputs:
- gains: float32 [8, 2, 32, 512], P('band', None, None, 'dir')
- coefficients: float32 [3, 2, 32, 512], P(None, None, None, 'dir')
- residual: float32 [8, 2, 512, 512], P('band', None, 'dir')
Inputs may be any that keep to these rules, and one draw needn't show every extreme that they name: `counts`: every direction has at least 512 live source slots, and some direction has exactly 1536.
All inputs are finite; a program needn't handle non-finite values.
Results may differ from a plain program's by a relative error of at most 0.0024.
Values may be sent and summed in bfloat16 or wider, within the bound.
A program may use at most 64 MiB of HBM per device.

v0:
```python
import jax
import jax.numpy as jnp
from jax import lax
from jax.sharding import PartitionSpec as P

SWEEPS = 3


RIDGE_WEIGHT = 0.25
DAMPING = 0.5


def gram_inverse(band_total):
    locations = [(2.0 * position + 1.0 - band_total) / band_total for position in range(band_total)]
    gram = [
        [
            sum((location ** (first_index + second_index) for location in locations))
            + (RIDGE_WEIGHT if first_index == second_index else 0.0)
            for second_index in range(3)
        ]
        for first_index in range(3)
    ]

    def cofactor(first_index, second_index):
        kept_rows = [index_value for index_value in range(3) if index_value != first_index]
        kept_cols = [index_value for index_value in range(3) if index_value != second_index]
        minor_value = (
            gram[kept_rows[0]][kept_cols[0]] * gram[kept_rows[1]][kept_cols[1]]
            - gram[kept_rows[0]][kept_cols[1]] * gram[kept_rows[1]][kept_cols[0]]
        )
        return minor_value if (first_index + second_index) % 2 == 0 else -minor_value

    determinant = sum((gram[0][column] * cofactor(0, column) for column in range(3)))
    return [
        [cofactor(column, row_index) / determinant for column in range(3)] for row_index in range(3)
    ]


def basis_terms(position, band_total):
    frequency = (2.0 * position + 1.0 - band_total) / band_total
    return [jnp.ones_like(frequency), frequency, frequency * frequency]


def contract(left, right):
    return lax.dot_general(
        left, right, (((1,), (1,)), ((), ())), preferred_element_type=jnp.float32
    )


def project(coherency, row_gains, column_gains):
    coh_real = coherency[:, 0].astype(jnp.float32)
    coh_imag = coherency[:, 1].astype(jnp.float32)
    column_real = column_gains[0][:, None, :]
    column_imag = column_gains[1][:, None, :]
    along_real = coh_real * column_real + coh_imag * column_imag
    along_imag = coh_imag * column_real - coh_real * column_imag
    row_real = row_gains[0][:, :, None]
    row_imag = row_gains[1][:, :, None]
    model_real = jnp.sum(row_real * along_real - row_imag * along_imag, axis=0)
    model_imag = jnp.sum(row_real * along_imag + row_imag * along_real, axis=0)
    return (along_real, along_imag, model_real, model_imag)


def solve(
    along_real, along_imag, resid_real, resid_imag, offdiag, row_gains, target, duals, penalty
):
    weight_sum = jnp.sum(
        (along_real * along_real + along_imag * along_imag) * offdiag[None], axis=2
    )
    numer_real = (
        jnp.sum(resid_real[None] * along_real + resid_imag[None] * along_imag, axis=2)
        + row_gains[0] * weight_sum
    )
    numer_imag = (
        jnp.sum(resid_imag[None] * along_real - resid_real[None] * along_imag, axis=2)
        + row_gains[1] * weight_sum
    )
    strength = penalty[:, None]
    solved_real = (numer_real + strength * (target[0] - duals[0])) / (weight_sum + strength)
    solved_imag = (numer_imag + strength * (target[1] - duals[1])) / (weight_sum + strength)
    solved = jnp.stack([solved_real, solved_imag])
    return row_gains + DAMPING * (solved - row_gains)


def on_device(responses, fluxes, counts, penalty, visibilities, start_gains):
    response = responses[0, 0]
    source_flux = fluxes[0, 0]
    live_count = counts[0]
    station_count = response.shape[1]
    source_count = response.shape[2]
    live_mask = jnp.arange(source_count) < live_count
    weight = jnp.where(live_mask, source_flux, 0.0)
    stacked = response.reshape(2 * station_count, source_count)
    scaled = (stacked.astype(jnp.float32) * weight[None, :]).astype(jnp.bfloat16)
    product = contract(stacked, scaled)
    real_part = product[:station_count, :station_count] + product[station_count:, station_count:]
    imag_part = product[station_count:, :station_count] - product[:station_count, station_count:]
    coherency = jnp.stack([real_part, imag_part]).astype(jnp.bfloat16)[None]
    band_total = lax.axis_size("band")
    terms = basis_terms(lax.axis_index("band").astype(jnp.float32), float(band_total))
    inverse = gram_inverse(band_total)
    dir_index = lax.axis_index("dir")
    observed = visibilities[0]
    row_count = observed.shape[1]
    first_row = dir_index * row_count
    row_offdiag = (
        (first_row + jnp.arange(row_count))[:, None] != jnp.arange(station_count)[None, :]
    ).astype(jnp.float32)
    all_visibilities = lax.all_gather(observed, "dir", axis=1, tiled=True)
    full_offdiag = (
        jnp.arange(station_count)[:, None] != jnp.arange(station_count)[None, :]
    ).astype(jnp.float32)
    own_penalty = lax.dynamic_slice_in_dim(penalty, dir_index, 1)
    current = lax.all_to_all(start_gains[0], "dir", split_axis=1, concat_axis=2, tiled=True)
    target = current
    duals = jnp.zeros_like(current)
    coefficients = jnp.zeros((3,) + current.shape, jnp.float32)
    for repeat in range(SWEEPS):
        along_real, along_imag, model_real, model_imag = project(coherency, current, current)
        total_real, total_imag = lax.psum((model_real, model_imag), "dir")
        resid_real = (all_visibilities[0] - total_real) * full_offdiag
        resid_imag = (all_visibilities[1] - total_imag) * full_offdiag
        current = solve(
            along_real,
            along_imag,
            resid_real,
            resid_imag,
            full_offdiag,
            current,
            target,
            duals,
            own_penalty,
        )
        mixed = current + duals
        moments = lax.psum(jnp.stack([term * mixed for term in terms]), "band")
        coeff_list = [
            moments[0] * inverse[row_index][0]
            + moments[1] * inverse[row_index][1]
            + moments[2] * inverse[row_index][2]
            for row_index in range(3)
        ]
        consensus_target = (
            terms[0] * coeff_list[0] + terms[1] * coeff_list[1] + terms[2] * coeff_list[2]
        )
        coefficients = jnp.stack(coeff_list)
        target = consensus_target
        duals = duals + current - target
    along_real, along_imag, model_real, model_imag = project(coherency, current, current)
    model_rows = lax.psum_scatter(
        jnp.stack([model_real, model_imag]), "dir", scatter_dimension=1, tiled=True
    )
    residual = (observed - model_rows) * row_offdiag[None]
    packed = jnp.concatenate([current[None], coefficients], axis=0)
    regrouped = lax.all_to_all(packed, "dir", split_axis=3, concat_axis=2, tiled=True)
    return (regrouped[0][None], regrouped[1:], residual[None])


def solution(mesh):
    in_specs = (
        P("band", "dir", None, None, None),
        P("band", "dir", None),
        P("dir"),
        P(),
        P("band", None, "dir", None),
        P("band", None, None, "dir"),
    )
    out_specs = (
        P("band", None, None, "dir"),
        P(None, None, None, "dir"),
        P("band", None, "dir", None),
    )
    return jax.shard_map(
        on_device, mesh=mesh, in_specs=in_specs, out_specs=out_specs, check_vma=False
    )
```

profile of v0, /device:TPU:1, one launch (start us, length us, event | category | flops | bytes accessed | tf_op | source)
XLA Modules:
  0.0 1318.1 jit_solution(11361330160142440964)
XLA Ops:
  7.2 0.0 all-gather.3.cloned.1.call-start
  7.2 1.5 copy.39
  8.7 0.0 all-gather.3.cloned.1.call-update
  8.8 1.4 copy.37
  10.2 12.6 all-to-all-start
  22.8 0.0 all-reduce.15.cloned.1.call-start
  23.5 0.7 reduce.16
  24.2 2.6 multiply_convert_fusion
  26.8 0.2 copy-done
  27.0 5.0 convolution_bitcast_fusion
  32.0 0.4 all-to-all-done
  32.5 0.1 slice_reduce_fusion.1
  32.6 0.1 mul.1695
  32.6 0.1 mul.1689
  32.7 2.7 fusion.20
  35.5 1.9 multiply_add_fusion.3
  37.3 0.0 all-reduce.13.cloned.1.call-start
  37.4 0.6 dynamic_slice.3
  38.0 0.1 all_to_all.9
  38.1 0.1 all_to_all.20
  38.2 0.1 squeeze.22
  38.3 0.1 squeeze.23
  38.3 31.7 %all-gather.3.cloned.1.call-done = f32[1,2,512,512]{3,1,0,2:T(2,128)} async-done(((f32[1,2,16,512]{3,1,0,2:T(2,128)}), f32[1,2,512,512]{3,1,0,2:T(2,128)}) %all-gather.3.cloned.1.call-update) | async-done | bytes 2097168 | tf_op jit(solution)/shard_map/all_gather | solution.py:109
  70.1 5.0 fusion.87
  75.1 1.3 copy.53
  76.4 2.3 copy.54
  78.8 282.2 %all-reduce.15.cloned.1.call-done = (f32[512,512]{0,1:T(8,128)}, f32[512,512]{0,1:T(8,128)}) async-done(((f32[512,512]{0,1:T(8,128)}, f32[512,512]{0,1:T(8,128)}), (f32[512,512]{0,1:T(8,128)}, f32[512,512]{0,1:T(8,128)})) %all-reduce.15.cloned.1.call-update) | async-done | bytes 2097168 | tf_op jit(solution)/shard_map/psum | solution.py:120
  361.0 2.3 add_reduce_fusion.2
  363.3 0.7 add_divide_fusion.1
  364.0 26.7 %psum.67 = f32[3,2,1,512]{3,1,2,0:T(2,128)S(1)} all-reduce(f32[3,2,1,512]{3,1,2,0:T(2,128)S(1)} %pad_maximum_fusion.2), channel_id=1, replica_groups=mesh['band'=8,'dir'=32] {'band'}, use_global_device_ids=true, to_apply=%region_9.10 | all-reduce | flops 3072 | bytes 24576 | tf_op jit(solution)/shard_map/psum | solution.py:135
  390.7 1.8 multiply_add_fusion.2
  392.5 0.0 all-reduce.11.cloned.1.call-start
  392.6 0.5 fusion.27
  393.1 293.9 %all-reduce.13.cloned.1.call-done = (f32[512,512]{0,1:T(8,128)}, f32[512,512]{0,1:T(8,128)}) async-done(((f32[512,512]{0,1:T(8,128)}, f32[512,512]{0,1:T(8,128)}), (f32[512,512]{0,1:T(8,128)}, f32[512,512]{0,1:T(8,128)})) %all-reduce.13.cloned.1.call-update) | async-done | bytes 2097168 | tf_op jit(solution)/shard_map/psum | solution.py:120
  687.0 2.3 add_reduce_fusion.1
  689.2 0.7 fusion.77
  690.0 26.7 %psum.70 = f32[3,2,1,512]{3,1,2,0:T(2,128)S(1)} all-reduce(f32[3,2,1,512]{3,1,2,0:T(2,128)S(1)} %pad_maximum_fusion.3), channel_id=1, replica_groups=mesh['band'=8,'dir'=32] {'band'}, use_global_device_ids=true, to_apply=%region_15.16 | all-reduce | flops 3072 | bytes 24576 | tf_op jit(solution)/shard_map/psum | solution.py:135
  716.7 1.8 multiply_add_fusion.1
  718.5 0.2 all-reduce.9.cloned.1.call-start
  718.8 0.5 fusion.34
  719.3 293.9 %all-reduce.11.cloned.1.call-done = (f32[512,512]{0,1:T(8,128)}, f32[512,512]{0,1:T(8,128)}) async-done(((f32[512,512]{0,1:T(8,128)}, f32[512,512]{0,1:T(8,128)}), (f32[512,512]{0,1:T(8,128)}, f32[512,512]{0,1:T(8,128)})) %all-reduce.11.cloned.1.call-update) | async-done | bytes 2097168 | tf_op jit(solution)/shard_map/psum | solution.py:120
  1013.2 2.3 add_reduce_fusion
  1015.5 0.7 fusion.79
  1016.2 0.6 multiply_subtract_fusion
  1016.7 0.2 pad_maximum_fusion
  1016.9 2.5 copy.47
  1019.5 27.6 %psum.71 = f32[3,2,1,512]{3,1,2,0:T(2,128)S(1)} all-reduce(f32[3,2,1,512]{3,1,2,0:T(2,128)S(1)} %pad_maximum_fusion.4), channel_id=1, replica_groups=mesh['band'=8,'dir'=32] {'band'}, use_global_device_ids=true, to_apply=%region_17.18 | all-reduce | flops 3072 | bytes 24576 | tf_op jit(solution)/shard_map/psum | solution.py:135
  1047.1 0.3 copy.43
  1047.4 1.3 reshape.2883
  1048.7 13.2 all-to-all-start.1
  1061.9 0.1 fusion.55
  1062.0 0.6 dynamic-slice
  1063.2 8.0 all-to-all-done.1
  1071.2 0.5 broadcast.1645
  1071.7 0.7 reduce.28
  1072.4 0.8 reshape.2884
  1073.2 0.6 slice.225
  1073.8 0.2 copy.44
  1074.0 0.1 slice.184
  1074.1 0.7 copy.48
  1074.8 1.0 copy.49
  1075.8 234.2 %all-reduce.9.cloned.1.call-done = f32[2,512,512]{2,0,1:T(2,128)} async-done(((f32[2,512,512]{2,0,1:T(2,128)}), f32[2,512,512]{2,0,1:T(2,128)}) %all-reduce.9.cloned.1.call-update) | async-done | bytes 2097168
  1310.0 0.9 fusion.54
  1311.0 0.6 copy.50
  (31 shorter events, 0.3 us)
Async XLA Ops:
  7.2 62.9 %all-gather.3.cloned.1.call-start = ((), (), s32[]{:S(2)}) async-start(), calls=%async_computation.2 | async-start | bytes 2162688 | tf_op jit(solution)/shard_map/all_gather | solution.py:109
  10.2 22.3 %all-to-all-start = ((f32[2,32,16]{2,0,1:T(2,128)}), f32[2,32,16]{2,0,1:T(2,128)S(1)}, u32[]{:S(2)}, u32[]{:S(2)}) async-start(f32[2,32,16]{2,0,1:T(2,128)} %bitcast), calls=%async_computation | async-start | bytes 65536 | tf_op jit(solution)/shard_map/all_to_all | solution.py:114
  22.8 338.2 %all-reduce.15.cloned.1.call-start = ((), (), s32[]{:S(2)}) async-start(), calls=%async_computation.6 | async-start | bytes 4194304 | tf_op jit(solution)/shard_map/psum | solution.py:120
  24.2 2.8 copy-start
  35.5 2.0 copy-start.2
  37.3 649.6 %all-reduce.13.cloned.1.call-start = ((), (), s32[]{:S(2)}) async-start(), calls=%async_computation.5 | async-start | bytes 4194304 | tf_op jit(solution)/shard_map/psum | solution.py:120
  392.5 620.7 %all-reduce.11.cloned.1.call-start = ((), (), s32[]{:S(2)}) async-start(), calls=%async_computation.4 | async-start | bytes 4194304 | tf_op jit(solution)/shard_map/psum | solution.py:120
  718.5 591.5 %all-reduce.9.cloned.1.call-start = ((), (), s32[]{:S(2)}) async-start(), calls=%async_computation.3 | async-start | bytes 4194304
  1016.9 45.0 %copy-start.3 = (u32[256]{0:T(256)S(1)}, u32[256]{0:T(256)}, u32[]{:S(2)}) copy-start(u32[256]{0:T(256)} %constant.56) | copy-start | bytes 3076
  1019.4 290.7 %copy-start.1 = (f32[1,2,16,512]{3,2,1,0:T(8,128)S(1)}, f32[1,2,16,512]{3,2,1,0:T(8,128)}, u32[]{:S(2)}) copy-start(f32[1,2,16,512]{3,2,1,0:T(8,128)} %param.10) | copy-start | bytes 196612
  1048.7 22.5 %all-to-all-start.1 = ((f32[32,1,128]{2,1,0:T(1,128)}), f32[32,1,128]{2,1,0:T(1,128)S(1)}, u32[]{:S(2)}, u32[]{:S(2)}) async-start(f32[32,1,128]{2,1,0:T(1,128)} %reshape.2883), calls=%async_computation.1 | async-start | bytes 32768 | tf_op jit(solution)/shard_map/all_to_all | solution.py:154
Sparse Core Ops, SparseCore 0:
  11.1 58.8 all-gather.2
  72.7 288.2 all-reduce.14
  392.6 294.2 all-reduce.12
  718.7 294.4 all-reduce.10
  1019.5 290.4 all-reduce.8
where the time goes:
time: 1320 us
  waiting for transfers between devices  1140 us (86%)
  blocking collectives  80.9 us (6%)
  starting transfers between devices  26.1 us (2%)
  other arithmetic  24 us (2%)
  local copies, waits for them, and re-layouts  22.2 us (2%)
  between operations  15.4 us (1%)
    psum x3, waiting for transfers between devices, on_device(): total_real, total_imag = lax.psum((model_real, model_imag), 'dir')  870 us
    unnamed x6, waiting for transfers between devices  234 us
    psum x3, blocking collectives, on_device(): moments = lax.psum(jnp.stack([term * mixed for term in terms]), 'band')  80.9 us
    all_gather x1, waiting for transfers between devices, on_device(): all_visibilities = lax.all_gather(observed, 'dir', axis=1, tiled=True)  31.7 us
  transfers between devices with their start and end apart: 7, of which 7 were waited for; matrix products, arithmetic and copies ran while one was open for 2% of the time, Pallas kernels for 0%

commit v1 on v0

v1 whole, which is shorter than its diff:
```python
import functools

import jax
import jax.numpy as jnp
from jax import lax
from jax.experimental import pallas as pl
from jax.experimental.pallas import tpu as pltpu
from jax.sharding import PartitionSpec as P

MESH = pl.DeviceIdType.MESH
SWEEPS = 3
RIDGE_WEIGHT = 0.25
DAMPING = 0.5
SLABS = 4
PART = 32
GROUP = 8
NT = (((1,), (1,)), ((), ()))


def gram_inverse(band_total):
    locations = [(2.0 * position + 1.0 - band_total) / band_total for position in range(band_total)]
    gram = [
        [
            sum((location ** (first + second) for location in locations))
            + (RIDGE_WEIGHT if first == second else 0.0)
            for second in range(3)
        ]
        for first in range(3)
    ]

    def cofactor(first, second):
        rows = [index for index in range(3) if index != first]
        cols = [index for index in range(3) if index != second]
        minor = gram[rows[0]][cols[0]] * gram[rows[1]][cols[1]] - gram[rows[0]][cols[1]] * gram[rows[1]][cols[0]]
        return minor if (first + second) % 2 == 0 else -minor

    determinant = sum((gram[0][column] * cofactor(0, column) for column in range(3)))
    return [[cofactor(column, row) / determinant for column in range(3)] for row in range(3)]


def calibrate(
    n_band,
    n_dir,
    resp_any,
    flux_ref,
    count_ref,
    penalty_ref,
    vis_ref,
    start_ref,
    gains_ref,
    coeff_ref,
    resid_ref,
    resp,
    scaled,
    coh_out,
    coh_in,
    coh,
    along,
    columns,
    rows_wide,
    gain_out,
    gain_in,
    mixed_out,
    mixed_in,
    load_sem,
    coh_send,
    coh_recv,
    gain_send,
    gain_recv,
    mixed_send,
    mixed_recv,
):
    me = lax.axis_index("dir")
    band = lax.axis_index("band")
    stations, sources = resp.shape[1], resp.shape[2]
    per_slab = n_dir // SLABS
    own = stations // n_dir
    tiles = stations // 128
    slab_rows = stations // SLABS
    my_slab = me // per_slab
    my_place = lax.rem(me, per_slab)

    load = pltpu.make_async_copy(resp_any.at[0, 0], resp, load_sem)
    load.start()

    barrier = pltpu.get_barrier_semaphore()

    def greet_dir(step, carry):
        pl.semaphore_signal(
            barrier, inc=1, device_id=(band, lax.rem(me + step, n_dir)), device_id_type=MESH
        )
        return carry

    def greet_band(step, carry):
        pl.semaphore_signal(
            barrier, inc=1, device_id=(lax.rem(band + step, n_band), me), device_id_type=MESH
        )
        return carry

    lax.fori_loop(1, n_dir, greet_dir, 0)
    lax.fori_loop(1, n_band, greet_band, 0)

    lane = lax.broadcasted_iota(jnp.int32, (own, 128), 1)
    dir_lane = lane % PART
    part_lane = lane % (2 * PART)
    low_half = lane < 2 * PART
    fold = (
        lax.broadcasted_iota(jnp.int32, (2 * PART, 128), 0)
        == lax.broadcasted_iota(jnp.int32, (2 * PART, 128), 1) % (2 * PART)
    ).astype(jnp.bfloat16)

    def split(value):
        high = value.astype(jnp.bfloat16).astype(jnp.float32)
        return jnp.where(low_half, high, value - high).astype(jnp.bfloat16)

    def unpack(value):
        return lax.dot_general(fold, value, NT, preferred_element_type=jnp.float32)

    eye = (
        lax.broadcasted_iota(jnp.int32, (own, own), 0) == lax.broadcasted_iota(jnp.int32, (own, own), 1)
    ).astype(jnp.bfloat16)
    pieces = []
    for part in range(2):
        pieces.append(start_ref[0, part])
        if n_dir < PART:
            pieces.append(jnp.zeros((PART - n_dir, own), jnp.float32))
    stacked = jnp.concatenate(pieces + pieces, axis=0)
    first = stacked.astype(jnp.bfloat16)
    rest = stacked - first.astype(jnp.float32)
    second = rest.astype(jnp.bfloat16)
    third = (rest - second.astype(jnp.float32)).astype(jnp.bfloat16)
    gains = (
        lax.dot_general(eye, first, NT, preferred_element_type=jnp.float32)
        + lax.dot_general(eye, second, NT, preferred_element_type=jnp.float32)
    ) + lax.dot_general(eye, third, NT, preferred_element_type=jnp.float32)

    strength = jnp.ones((own, 128), jnp.float32)
    for index in range(n_dir):
        strength = jnp.where(dir_lane == index, penalty_ref[index], strength)

    row_id = lax.broadcasted_iota(jnp.int32, (own, stations), 0) + me * own
    col_id = lax.broadcasted_iota(jnp.int32, (own, stations), 1)
    vis_re = jnp.where(row_id == col_id, 0.0, vis_ref[0, 0])
    vis_im = jnp.where(row_id == col_id, 0.0, vis_ref[0, 1])

    def tile(value, index):
        return value[:, index * 128 : (index + 1) * 128]

    def widen(value):
        for part in range(2):
            for index in range(n_dir):
                place = part * PART + index
                rows_wide[place] = jnp.broadcast_to(value[:, place : place + 1], (own, 128))

    def send_gains(slot, value):
        gain_out[slot] = split(value)
        gain_in[slot, me] = gain_out[slot]

        def send(step, carry):
            peer = lax.rem(me + step, n_dir)
            pltpu.make_async_remote_copy(
                src_ref=gain_out.at[slot],
                dst_ref=gain_in.at[slot, me],
                send_sem=gain_send.at[slot],
                recv_sem=gain_recv.at[slot],
                device_id=(band, peer),
                device_id_type=MESH,
            ).start()
            return carry

        lax.fori_loop(1, n_dir, send, 0)

    def receive_gains(slot):
        whole = gain_in.at[slot, pl.ds(0, n_dir - 1)]
        pltpu.make_async_copy(whole, whole, gain_recv.at[slot]).wait()
        packed = gain_in[slot].reshape(n_dir * own, 128)
        columns[...] = unpack(packed).reshape(columns.shape)

    def send_mixed(slot, value):
        mixed_out[slot] = split(value)
        mixed_in[slot, band] = mixed_out[slot]

        def send(step, carry):
            peer = lax.rem(band + step, n_band)
            pltpu.make_async_remote_copy(
                src_ref=mixed_out.at[slot],
                dst_ref=mixed_in.at[slot, band],
                send_sem=mixed_send.at[slot],
                recv_sem=mixed_recv.at[slot],
                device_id=(peer, me),
                device_id_type=MESH,
            ).start()
            return carry

        lax.fori_loop(1, n_band, send, 0)

    inverse = gram_inverse(n_band)
    own_place = (2.0 * band.astype(jnp.float32) + 1.0 - n_band) / n_band

    def receive_mixed(slot):
        whole = mixed_in.at[slot, pl.ds(0, n_band - 1)]
        pltpu.make_async_copy(whole, whole, mixed_recv.at[slot]).wait()
        sums = [None, None, None]
        for index in range(n_band):
            place = (2.0 * index + 1.0 - n_band) / n_band
            value = mixed_in[slot, index].astype(jnp.float32)
            for order in range(3):
                term = value * (place**order)
                sums[order] = term if sums[order] is None else sums[order] + term
        moments = [value + pltpu.roll(value, 2 * PART, 1) for value in sums]
        return [
            moments[0] * inverse[row][0] + moments[1] * inverse[row][1] + moments[2] * inverse[row][2]
            for row in range(3)
        ]

    live = lax.broadcasted_iota(jnp.int32, (1, sources), 1) < count_ref[0]
    weight = jnp.where(live, flux_ref[0], 0.0)
    load.wait()
    chunk = 64

    def scale(step, carry):
        for part in range(2):
            begin = pl.multiple_of(step * chunk, chunk)
            block = resp[part, pl.ds(begin, chunk), :].astype(jnp.float32)
            scaled[pl.ds(pl.multiple_of(part * stations + begin, chunk), chunk), :] = (
                block * weight
            ).astype(jnp.bfloat16)
        return carry

    lax.fori_loop(0, stations // chunk, scale, 0)

    def slab_step(step, carry):
        slab = lax.rem(my_slab + 2 + 3 * step + 3 * (step // 2) + 2 * (step // 3), SLABS)
        begin = pl.multiple_of(slab * slab_rows, slab_rows)
        left = jnp.concatenate(
            [resp[0, pl.ds(begin, slab_rows), :], resp[1, pl.ds(begin, slab_rows), :]], axis=0
        )
        by_re = lax.dot_general(left, scaled[:stations], NT, preferred_element_type=jnp.float32)
        by_im = lax.dot_general(left, scaled[stations:], NT, preferred_element_type=jnp.float32)
        real = by_re[:slab_rows] + by_im[slab_rows:]
        imag = by_re[slab_rows:] - by_im[:slab_rows]
        off = (lax.broadcasted_iota(jnp.int32, (slab_rows, stations), 0) + begin) != (
            lax.broadcasted_iota(jnp.int32, (slab_rows, stations), 1)
        )
        shape = (per_slab, own, stations)
        first_dir = slab * per_slab
        coh_out[pl.ds(first_dir, per_slab), 0] = (
            jnp.where(off, real, 0.0).astype(jnp.bfloat16).reshape(shape)
        )
        coh_out[pl.ds(first_dir, per_slab), 1] = (
            jnp.where(off, imag, 0.0).astype(jnp.bfloat16).reshape(shape)
        )

        @pl.when(step == 0)
        def _():
            pl.semaphore_wait(barrier, n_dir + n_band - 2)
            send_gains(0, gains)

        def send(place, inner):
            peer = first_dir + lax.rem(my_place + place, per_slab)

            @pl.when(peer != me)
            def _():
                pltpu.make_async_remote_copy(
                    src_ref=coh_out.at[peer],
                    dst_ref=coh_in.at[me],
                    send_sem=coh_send,
                    recv_sem=coh_recv.at[me],
                    device_id=(band, peer),
                    device_id_type=MESH,
                ).start()

            return inner

        lax.fori_loop(0, per_slab, send, 0)
        return carry

    lax.fori_loop(0, SLABS, slab_step, 0)
    coh_in[me] = coh_out[me]

    zero = jnp.zeros((own, 128), jnp.float32)

    def project(arriving):
        def step(group, totals):
            out = list(totals)
            for member in range(GROUP):
                index = group * GROUP + member
                if arriving:

                    @pl.when(index != me)
                    def _(index=index):
                        block = coh_in.at[index]
                        pltpu.make_async_copy(block, block, coh_recv.at[index]).wait()

                    coh[index] = coh_in[index].astype(jnp.float32)
                row_re = rows_wide[index]
                row_im = rows_wide[PART + index]
                for place in range(tiles):
                    here = pl.ds(place * 128, 128)
                    coh_re = coh[index, 0, :, here]
                    coh_im = coh[index, 1, :, here]
                    col_re = columns[group, member : member + 1, here]
                    col_im = columns[PART // GROUP + group, member : member + 1, here]
                    along_re = coh_re * col_re + coh_im * col_im
                    along_im = coh_im * col_re - coh_re * col_im
                    along[index, 0, :, here] = along_re
                    along[index, 1, :, here] = along_im
                    out[2 * place] += row_re * along_re - row_im * along_im
                    out[2 * place + 1] += row_re * along_im + row_im * along_re
            return tuple(out)

        totals = lax.fori_loop(0, n_dir // GROUP, step, (zero,) * (2 * tiles))
        return (
            [tile(vis_re, place) - totals[2 * place] for place in range(tiles)],
            [tile(vis_im, place) - totals[2 * place + 1] for place in range(tiles)],
        )

    def reduce(residual_re, residual_im):
        def step(index, carry):
            numer, weights = carry
            total_re, total_im, total_weight = zero, zero, zero
            for place in range(tiles):
                here = pl.ds(place * 128, 128)
                along_re = along[index, 0, :, here]
                along_im = along[index, 1, :, here]
                total_weight += along_re * along_re + along_im * along_im
                total_re += residual_re[place] * along_re + residual_im[place] * along_im
                total_im += residual_im[place] * along_re - residual_re[place] * along_im
            sum_re = jnp.sum(total_re, axis=1, keepdims=True)
            sum_im = jnp.sum(total_im, axis=1, keepdims=True)
            sum_weight = jnp.sum(total_weight, axis=1, keepdims=True)
            numer = jnp.where(
                part_lane == index, sum_re, jnp.where(part_lane == PART + index, sum_im, numer)
            )
            weights = jnp.where(dir_lane == index, sum_weight, weights)
            return numer, weights

        return lax.fori_loop(0, n_dir, step, (zero, zero))

    target = gains
    duals = zero
    coefficients = None
    for sweep in range(SWEEPS):
        widen(gains)
        receive_gains(sweep)
        residual_re, residual_im = project(sweep == 0)
        numer, weights = reduce(residual_re, residual_im)
        if sweep > 0:
            coefficients = receive_mixed(sweep - 1)
            target = coefficients[0] + own_place * coefficients[1] + own_place * own_place * coefficients[2]
            duals = duals + gains - target
        solved = (numer + gains * weights + strength * (target - duals)) / (weights + strength)
        gains = gains + DAMPING * (solved - gains)
        send_gains(sweep + 1, gains)
        send_mixed(sweep, gains + duals)
    widen(gains)
    own_gains = unpack(gain_out[SWEEPS])
    for part in range(2):
        gains_ref[0, part] = own_gains[part * PART : part * PART + n_dir]
    receive_gains(SWEEPS)
    residual_re, residual_im = project(False)
    for place in range(tiles):
        here = pl.ds(place * 128, 128)
        resid_ref[0, 0, :, here] = residual_re[place]
        resid_ref[0, 1, :, here] = residual_im[place]
    coefficients = receive_mixed(SWEEPS - 1)
    for order in range(3):
        value = unpack(split(coefficients[order]))
        for part in range(2):
            coeff_ref[order, part] = value[part * PART : part * PART + n_dir]

    whole = coh_out.at[pl.ds(0, n_dir - 1)]
    pltpu.make_async_copy(whole, whole, coh_send).wait()
    for slot in range(SWEEPS + 1):
        whole = gain_in.at[slot, pl.ds(0, n_dir - 1)]
        pltpu.make_async_copy(whole, whole, gain_send.at[slot]).wait()
    for slot in range(SWEEPS):
        whole = mixed_in.at[slot, pl.ds(0, n_band - 1)]
        pltpu.make_async_copy(whole, whole, mixed_send.at[slot]).wait()


def on_device(n_band, n_dir, responses, fluxes, counts, penalty, visibilities, start_gains):
    stations, sources = responses.shape[3], responses.shape[4]
    own = stations // n_dir
    vmem = pl.BlockSpec(memory_space=pltpu.VMEM)
    smem = pl.BlockSpec(memory_space=pltpu.SMEM)
    bf16, f32 = jnp.bfloat16, jnp.float32
    return pl.pallas_call(
        functools.partial(calibrate, n_band, n_dir),
        out_shape=(
            jax.ShapeDtypeStruct((1, 2, n_dir, own), f32),
            jax.ShapeDtypeStruct((3, 2, n_dir, own), f32),
            jax.ShapeDtypeStruct((1, 2, own, stations), f32),
        ),
        in_specs=[pl.BlockSpec(memory_space=pl.ANY), vmem, smem, smem, vmem, vmem],
        out_specs=(vmem, vmem, vmem),
        scratch_shapes=[
            pltpu.VMEM((2, stations, sources), bf16),
            pltpu.VMEM((2 * stations, sources), bf16),
            pltpu.VMEM((n_dir, 2, own, stations), bf16),
            pltpu.VMEM((n_dir, 2, own, stations), bf16),
            pltpu.VMEM((n_dir, 2, own, stations), f32),
            pltpu.VMEM((n_dir, 2, own, stations), f32),
            pltpu.VMEM((2 * PART // GROUP, GROUP, stations), f32),
            pltpu.VMEM((2 * PART, own, 128), f32),
            pltpu.VMEM((SWEEPS + 1, own, 128), bf16),
            pltpu.VMEM((SWEEPS + 1, n_dir, own, 128), bf16),
            pltpu.VMEM((SWEEPS, own, 128), bf16),
            pltpu.VMEM((SWEEPS, n_band, own, 128), bf16),
            pltpu.SemaphoreType.DMA,
            pltpu.SemaphoreType.DMA,
            pltpu.SemaphoreType.DMA((n_dir,)),
            pltpu.SemaphoreType.DMA((SWEEPS + 1,)),
            pltpu.SemaphoreType.DMA((SWEEPS + 1,)),
            pltpu.SemaphoreType.DMA((SWEEPS,)),
            pltpu.SemaphoreType.DMA((SWEEPS,)),
        ],
        compiler_params=pltpu.CompilerParams(
            collective_id=0, has_side_effects=True, vmem_limit_bytes=40 * 1024 * 1024
        ),
    )(responses, fluxes, counts, penalty, visibilities, start_gains)


def solution(mesh):
    in_specs = (
        P("band", "dir", None, None, None),
        P("band", "dir", None),
        P("dir"),
        P(),
        P("band", None, "dir", None),
        P("band", None, None, "dir"),
    )
    out_specs = (
        P("band", None, None, "dir"),
        P(None, None, None, "dir"),
        P("band", None, "dir", None),
    )
    return jax.shard_map(
        functools.partial(on_device, mesh.shape["band"], mesh.shape["dir"]),
        mesh=mesh,
        in_specs=in_specs,
        out_specs=out_specs,
        check_vma=False,
    )
```

time: 1320 us -> 82.1 us (0.06)
  waiting for transfers between devices: 1140 us -> 0 us
  blocking collectives: 80.9 us -> 0 us
  Pallas kernels: 0 us -> 73.7 us
  starting transfers between devices: 26.1 us -> 0 us
  other arithmetic: 24 us -> 0 us
  local copies, waits for them, and re-layouts: 22.2 us -> 6.88 us
  between operations: 15.4 us -> 1.29 us
    psum x3 -> x0, waiting for transfers between devices: 870 us -> none  [on_device(): total_real, total_imag = lax.psum((model_real, model_imag), 'dir')]
    unnamed x6 -> x0, waiting for transfers between devices: 234 us -> none
    psum x3 -> x0, blocking collectives: 80.9 us -> none  [on_device(): moments = lax.psum(jnp.stack([term * mixed for term in terms]), 'band')]
    pallas_call x0 -> x1, Pallas kernels: none -> 73.7 us  [on_device(): pl.pallas_call(functools.partial(calibrate, n_band, n_dir), out_shape=(ja...]
    all_gather x1 -> x0, waiting for transfers between devices: 31.7 us -> none  [on_device(): all_visibilities = lax.all_gather(observed, 'dir', axis=1, tiled=True)]
    all_to_all x2 -> x0, starting transfers between devices: 25.7 us -> none  [the longest x1 13.2 us: on_device(): lax.all_to_all(packed, 'dir', split_axis=3, concat_axis=2, tiled=True)]
  transfers between devices with their start and end apart: 7 -> 0, of which waited for: 7 -> 0; matrix products, arithmetic and copies ran while one was open for 2% -> 0% of each run, Pallas kernels for 0% -> 0%
where the time goes in v1:
time: 82.1 us; the launch traced here: 81.9 us
  Pallas kernels  73.7 us (90%)
  local copies, waits for them, and re-layouts  6.88 us (8%)
  between operations  1.29 us (2%)
    pallas_call x1, Pallas kernels, on_device(): pl.pallas_call(functools.partial(calibrate, n_band, n_dir), out_shape=(ja...  73.7 us
    unnamed x10, local copies, waits for them, and re-layouts  5.5 us

profile of v1, /device:TPU:1, one launch (start us, length us, event | category | flops | bytes accessed | tf_op | source)
XLA Modules:
  0.0 81.9 jit_solution(13767038145675315695)
XLA Ops:
  1.3 0.8 copy.9.start_ref
  2.1 0.0 copy-start
  2.1 1.9 %copy-done = bf16[1,1,2,512,1536]{4,3,2,1,0:T(8,128)(2,1)S(1)} copy-done((bf16[1,1,2,512,1536]{4,3,2,1,0:T(8,128)(2,1)S(1)}, bf16[1,1,2,512,1536]{4,3,2,1,0:T(8,128)(2,1)}, u32[]{:S(2)}) %copy-start) | copy-done | bytes 3145752
  4.0 0.0 copy-start.1
  4.0 0.8 %copy-done.1 = f32[1,2,16,512]{3,2,1,0:T(8,128)S(1)} copy-done((f32[1,2,16,512]{3,2,1,0:T(8,128)S(1)}, f32[1,2,16,512]{3,2,1,0:T(8,128)}, u32[]{:S(2)}) %copy-start.1) | copy-done | bytes 65560
  4.8 0.0 copy-start.2
  4.8 0.7 copy-done.2
  5.5 0.0 copy-start.3
  5.5 0.7 copy-done.3
  6.1 73.7 %shard_map.85 = (f32[1,2,32,16]{3,2,1,0:T(8,128)S(1)}, f32[3,2,32,16]{3,2,1,0:T(8,128)S(1)}, f32[1,2,16,512]{3,2,1,0:T(8,128)S(1)}) custom-call(bf16[1,1,2,512,1536]{4,3,2,1,0:T(8,128)(2,1)S(1)} %copy-done, f32[1,1,1536]{2,1,0:T(1,128)S(1)} %copy-done.2, s32[1]{0:T(128)S(6)} %copy.13.count_ref, f32[32]{0:T(128)S(1)} %copy-done.3, ...), custom_call_target="tpu_custom_call" | custom-call | tf_op jit(solution)/shard_map/pallas_call | solution.py:388
  79.9 0.7 copy.10
  80.5 0.7 copy.11
  81.2 0.6 copy.14
Async XLA Ops:
  2.1 1.9 %copy-start = (bf16[1,1,2,512,1536]{4,3,2,1,0:T(8,128)(2,1)S(1)}, bf16[1,1,2,512,1536]{4,3,2,1,0:T(8,128)(2,1)}, u32[]{:S(2)}) copy-start(bf16[1,1,2,512,1536]{4,3,2,1,0:T(8,128)(2,1)} %resp_any.1) | copy-start | bytes 9437188
  4.0 0.8 %copy-start.1 = (f32[1,2,16,512]{3,2,1,0:T(8,128)S(1)}, f32[1,2,16,512]{3,2,1,0:T(8,128)}, u32[]{:S(2)}) copy-start(f32[1,2,16,512]{3,2,1,0:T(8,128)} %vis_ref.1) | copy-start | bytes 196612
  4.8 0.7 copy-start.2
  5.5 0.7 copy-start.3

commit v2 on v1

v2 whole, which is shorter than its diff:
```python
import functools

import jax
import jax.numpy as jnp
from jax import lax
from jax.experimental import pallas as pl
from jax.experimental.pallas import tpu as pltpu
from jax.sharding import PartitionSpec as P

MESH = pl.DeviceIdType.MESH
SWEEPS = 3
RIDGE_WEIGHT = 0.25
DAMPING = 0.5
SLABS = 4
PART = 32
GROUP = 8
NT = (((1,), (1,)), ((), ()))


def gram_inverse(band_total):
    locations = [(2.0 * position + 1.0 - band_total) / band_total for position in range(band_total)]
    gram = [
        [
            sum((location ** (first + second) for location in locations))
            + (RIDGE_WEIGHT if first == second else 0.0)
            for second in range(3)
        ]
        for first in range(3)
    ]

    def cofactor(first, second):
        rows = [index for index in range(3) if index != first]
        cols = [index for index in range(3) if index != second]
        minor = gram[rows[0]][cols[0]] * gram[rows[1]][cols[1]] - gram[rows[0]][cols[1]] * gram[rows[1]][cols[0]]
        return minor if (first + second) % 2 == 0 else -minor

    determinant = sum((gram[0][column] * cofactor(0, column) for column in range(3)))
    return [[cofactor(column, row) / determinant for column in range(3)] for row in range(3)]


def calibrate(
    n_band,
    n_dir,
    resp_hbm,
    flux_hbm,
    count_ref,
    penalty_ref,
    vis_hbm,
    start_hbm,
    gains_ref,
    coeff_ref,
    resid_ref,
    resp,
    flux,
    vis,
    start,
    scaled,
    coh_out,
    coh_in,
    coh,
    along,
    columns,
    rows_wide,
    sums,
    gain_out,
    gain_in,
    mixed_out,
    mixed_in,
    load_sem,
    coh_send,
    coh_recv,
    gain_send,
    gain_recv,
    mixed_send,
    mixed_recv,
):
    me = lax.axis_index("dir")
    band = lax.axis_index("band")
    stations, sources = resp.shape[1], resp.shape[2]
    per_slab = n_dir // SLABS
    own = stations // n_dir
    tiles = SLABS
    width = stations // SLABS
    my_slab = me // per_slab
    my_place = lax.rem(me, per_slab)

    loads = [
        pltpu.make_async_copy(source, goal, load_sem.at[index])
        for index, (source, goal) in enumerate(
            (
                (start_hbm.at[0], start),
                (flux_hbm.at[0], flux),
                (resp_hbm.at[0, 0], resp),
                (vis_hbm.at[0], vis),
            )
        )
    ]
    for load in loads:
        load.start()

    barrier = pltpu.get_barrier_semaphore()

    rotations = [step for step in (4, 5, 2, 3, 6, 7, 1, 0) if step < per_slab]
    places = [my_place if step == 0 else lax.rem(my_place + step, per_slab) for step in rotations]
    peers = []
    for offset in (2, 1, 3, 0):
        slab = lax.rem(my_slab + offset, SLABS)
        for step, place in zip(rotations, places):
            if offset or step:
                peers.append(slab * per_slab + place)
    bands = [lax.rem(band + step, n_band) for step in range(1, n_band)]
    for peer in peers:
        pl.semaphore_signal(barrier, inc=1, device_id=(band, peer), device_id_type=MESH)
    for peer in bands:
        pl.semaphore_signal(barrier, inc=1, device_id=(peer, me), device_id_type=MESH)

    lane = lax.broadcasted_iota(jnp.int32, (own, 128), 1)
    dir_lane = lane % PART
    part_lane = lane % (2 * PART)
    low_half = lane < 2 * PART
    fold = (
        lax.broadcasted_iota(jnp.int32, (2 * PART, 128), 0)
        == lax.broadcasted_iota(jnp.int32, (2 * PART, 128), 1) % (2 * PART)
    ).astype(jnp.bfloat16)
    zero = jnp.zeros((own, 128), jnp.float32)

    def split(value):
        high = value.astype(jnp.bfloat16).astype(jnp.float32)
        return jnp.where(low_half, high, value - high).astype(jnp.bfloat16)

    strength = jnp.ones((own, 128), jnp.float32)
    for index in range(n_dir):
        strength = jnp.where(dir_lane == index, penalty_ref[index], strength)

    loads[0].wait()
    pieces = []
    for part in range(2):
        pieces.append(start[part])
        if n_dir < PART:
            pieces.append(jnp.zeros((own, PART - n_dir), jnp.float32))
    gains = jnp.concatenate(pieces + pieces, axis=1)

    near = [lax.rem(my_slab + offset, SLABS) for offset in (0, 1, 3, 2)]
    spans = [pl.ds(pl.multiple_of(slab * width, width), width) for slab in near]

    def widen(value):
        for part in range(2):
            for index in range(n_dir):
                place = part * PART + index
                rows_wide[place] = jnp.broadcast_to(value[:, place : place + 1], (own, 128))

    def send_gains(slot, value):
        gain_out[slot] = split(value)
        gain_in[slot, my_slab, my_place] = gain_out[slot]

        for peer in peers:
            pltpu.make_async_remote_copy(
                src_ref=gain_out.at[slot],
                dst_ref=gain_in.at[slot, my_slab, my_place],
                send_sem=gain_send.at[slot],
                recv_sem=gain_recv.at[slot, my_slab],
                device_id=(band, peer),
                device_id_type=MESH,
            ).start()

    def receive_tile(slot, order):
        slab = near[order]
        whole = gain_in.at[slot, slab, pl.ds(0, per_slab - 1 if order == 0 else per_slab)]
        pltpu.make_async_copy(whole, whole, gain_recv.at[slot, slab]).wait()
        packed = gain_in[slot, slab].reshape(width, 128)
        value = lax.dot_general(fold, packed, NT, preferred_element_type=jnp.float32)
        columns[order] = value.reshape(columns.shape[1:])

    def send_mixed(slot, value):
        mixed_out[slot] = split(value)
        mixed_in[slot, band] = mixed_out[slot]

        for peer in bands:
            pltpu.make_async_remote_copy(
                src_ref=mixed_out.at[slot],
                dst_ref=mixed_in.at[slot, band],
                send_sem=mixed_send.at[slot],
                recv_sem=mixed_recv.at[slot],
                device_id=(peer, me),
                device_id_type=MESH,
            ).start()

    inverse = gram_inverse(n_band)
    own_place = (2.0 * band.astype(jnp.float32) + 1.0 - n_band) / n_band

    def receive_mixed(slot):
        whole = mixed_in.at[slot, pl.ds(0, n_band - 1)]
        pltpu.make_async_copy(whole, whole, mixed_recv.at[slot]).wait()
        totals = [None, None, None]
        for index in range(n_band):
            place = (2.0 * index + 1.0 - n_band) / n_band
            value = mixed_in[slot, index].astype(jnp.float32)
            for order in range(3):
                term = value * (place**order)
                totals[order] = term if totals[order] is None else totals[order] + term
        moments = [value + pltpu.roll(value, 2 * PART, 1) for value in totals]
        return [
            moments[0] * inverse[row][0] + moments[1] * inverse[row][1] + moments[2] * inverse[row][2]
            for row in range(3)
        ]

    loads[1].wait()
    live = lax.broadcasted_iota(jnp.int32, (1, sources), 1) < count_ref[0]
    weight = jnp.where(live, flux[...], 0.0)
    loads[2].wait()
    chunk = 64

    def scale(step, carry):
        for part in range(2):
            begin = pl.multiple_of(step * chunk, chunk)
            block = resp[part, pl.ds(begin, chunk), :].astype(jnp.float32)
            scaled[pl.ds(pl.multiple_of(part * stations + begin, chunk), chunk), :] = (
                block * weight
            ).astype(jnp.bfloat16)
        return carry

    lax.fori_loop(0, stations // chunk, scale, 0)

    def slab_step(step, carry):
        slab = lax.rem(my_slab + 2 + 3 * step + 3 * (step // 2) + 2 * (step // 3), SLABS)
        begin = pl.multiple_of(slab * width, width)
        left = jnp.concatenate([resp[0, pl.ds(begin, width), :], resp[1, pl.ds(begin, width), :]], axis=0)
        by_re = lax.dot_general(left, scaled[:stations], NT, preferred_element_type=jnp.float32)
        by_im = lax.dot_general(left, scaled[stations:], NT, preferred_element_type=jnp.float32)
        real = by_re[:width] + by_im[width:]
        imag = by_re[width:] - by_im[:width]
        off = (lax.broadcasted_iota(jnp.int32, (width, stations), 0) + begin) != (
            lax.broadcasted_iota(jnp.int32, (width, stations), 1)
        )
        shape = (per_slab, own, stations)
        first_dir = slab * per_slab
        coh_out[pl.ds(first_dir, per_slab), 0] = jnp.where(off, real, 0.0).astype(jnp.bfloat16).reshape(shape)
        coh_out[pl.ds(first_dir, per_slab), 1] = jnp.where(off, imag, 0.0).astype(jnp.bfloat16).reshape(shape)

        @pl.when(step == 0)
        def _():
            pl.semaphore_wait(barrier, n_dir + n_band - 2)
            send_gains(0, gains)

        def send(place, inner):
            peer = first_dir + lax.rem(my_place + per_slab // 2 + place, per_slab)

            @pl.when(peer != me)
            def _():
                pltpu.make_async_remote_copy(
                    src_ref=coh_out.at[peer],
                    dst_ref=coh_in.at[me],
                    send_sem=coh_send,
                    recv_sem=coh_recv.at[me],
                    device_id=(band, peer),
                    device_id_type=MESH,
                ).start()

            return inner

        lax.fori_loop(0, per_slab, send, 0)
        return carry

    lax.fori_loop(0, SLABS, slab_step, 0)
    coh_in[me] = coh_out[me]
    widen(gains)
    loads[3].wait()
    row_id = lax.broadcasted_iota(jnp.int32, (own, stations), 0) + me * own
    col_id = lax.broadcasted_iota(jnp.int32, (own, stations), 1)
    for part in range(2):
        vis[part] = jnp.where(row_id == col_id, 0.0, vis[part])

    def advance(index, group, member, order, totals):
        here = pl.ds(order * width, width)
        coh_re = coh[index, 0, :, here]
        coh_im = coh[index, 1, :, here]
        col_re = columns[order, group, member : member + 1]
        col_im = columns[order, PART // GROUP + group, member : member + 1]
        row_re = rows_wide[index]
        row_im = rows_wide[PART + index]
        along_re = coh_re * col_re + coh_im * col_im
        along_im = coh_im * col_re - coh_re * col_im
        along[index, 0, :, here] = along_re
        along[index, 1, :, here] = along_im
        return (
            totals[0] + (row_re * along_re - row_im * along_im),
            totals[1] + (row_re * along_im + row_im * along_re),
        )

    def left_over(order, totals):
        return vis[0, :, spans[order]] - totals[0], vis[1, :, spans[order]] - totals[1]

    def project_first():
        def step(group, totals):
            for member in range(GROUP):
                index = group * GROUP + member

                @pl.when(index != me)
                def _(index=index):
                    block = coh_in.at[index]
                    pltpu.make_async_copy(block, block, coh_recv.at[index]).wait()

                for order in range(tiles):
                    here = pl.ds(order * width, width)
                    for part in range(2):
                        coh[index, part, :, here] = coh_in[index, part, :, spans[order]].astype(jnp.float32)
                totals = tuple(
                    advance(index, group, member, order, totals[order]) for order in range(tiles)
                )
            return totals

        totals = lax.fori_loop(0, n_dir // GROUP, step, ((zero, zero),) * tiles)
        return [left_over(order, totals[order]) for order in range(tiles)]

    def project_tile(order):
        def step(group, totals):
            for member in range(GROUP):
                totals = advance(group * GROUP + member, group, member, order, totals)
            return totals

        return left_over(order, lax.fori_loop(0, n_dir // GROUP, step, (zero, zero)))

    def reduce(orders, residuals, opening, closing):
        def step(index, carry):
            if opening:
                total_re, total_im, total_weight = zero, zero, zero
            else:
                total_re, total_im, total_weight = sums[index, 0], sums[index, 1], sums[index, 2]
            for order, (residual_re, residual_im) in zip(orders, residuals):
                here = pl.ds(order * width, width)
                along_re = along[index, 0, :, here]
                along_im = along[index, 1, :, here]
                total_weight += along_re * along_re + along_im * along_im
                total_re += residual_re * along_re + residual_im * along_im
                total_im += residual_im * along_re - residual_re * along_im
            if not closing:
                sums[index, 0] = total_re
                sums[index, 1] = total_im
                sums[index, 2] = total_weight
                return carry
            numer, weights = carry
            sum_re = jnp.sum(total_re, axis=1, keepdims=True)
            sum_im = jnp.sum(total_im, axis=1, keepdims=True)
            sum_weight = jnp.sum(total_weight, axis=1, keepdims=True)
            numer = jnp.where(part_lane == index, sum_re, jnp.where(part_lane == PART + index, sum_im, numer))
            weights = jnp.where(dir_lane == index, sum_weight, weights)
            return numer, weights

        return lax.fori_loop(0, n_dir, step, (zero, zero), unroll=GROUP)

    target = gains
    duals = zero
    for sweep in range(SWEEPS):
        if sweep == 0:
            for order in range(tiles):
                receive_tile(0, order)
            numer, weights = reduce(range(tiles), project_first(), True, True)
        else:
            for order in range(tiles):
                receive_tile(sweep, order)
                residual = project_tile(order)
                numer, weights = reduce([order], [residual], order == 0, order == tiles - 1)
        solved = (numer + gains * weights + strength * (target - duals)) / (weights + strength)
        gains = gains + DAMPING * (solved - gains)
        send_gains(sweep + 1, gains)
        send_mixed(sweep, gains + duals)
        widen(gains)
        if sweep == SWEEPS - 1:
            for part in range(2):
                gains_ref[0, part] = gains[:, part * PART : part * PART + n_dir]
        coefficients = receive_mixed(sweep)
        target = coefficients[0] + own_place * coefficients[1] + own_place * own_place * coefficients[2]
        duals = duals + gains - target
    for order in range(3):
        for part in range(2):
            coeff_ref[order, part] = coefficients[order][:, part * PART : part * PART + n_dir]
    for order in range(tiles):
        receive_tile(SWEEPS, order)
        residual = project_tile(order)
        for part in range(2):
            resid_ref[0, part, :, spans[order]] = residual[part]

    whole = coh_out.at[pl.ds(0, n_dir - 1)]
    pltpu.make_async_copy(whole, whole, coh_send).wait()
    for slot in range(SWEEPS + 1):
        for slab in range(SLABS):
            whole = gain_in.at[slot, slab, pl.ds(0, per_slab - 1 if slab == 0 else per_slab)]
            pltpu.make_async_copy(whole, whole, gain_send.at[slot]).wait()
    for slot in range(SWEEPS):
        whole = mixed_in.at[slot, pl.ds(0, n_band - 1)]
        pltpu.make_async_copy(whole, whole, mixed_send.at[slot]).wait()


def on_device(n_band, n_dir, responses, fluxes, counts, penalty, visibilities, start_gains):
    stations, sources = responses.shape[3], responses.shape[4]
    own = stations // n_dir
    width = stations // SLABS
    per_slab = n_dir // SLABS
    hbm = pl.BlockSpec(memory_space=pltpu.HBM)
    vmem = pl.BlockSpec(memory_space=pltpu.VMEM)
    smem = pl.BlockSpec(memory_space=pltpu.SMEM)
    bf16, f32 = jnp.bfloat16, jnp.float32
    gains, coefficients, residual = pl.pallas_call(
        functools.partial(calibrate, n_band, n_dir),
        out_shape=(
            jax.ShapeDtypeStruct((1, 2, own, n_dir), f32),
            jax.ShapeDtypeStruct((3, 2, own, n_dir), f32),
            jax.ShapeDtypeStruct((1, 2, own, stations), f32),
        ),
        in_specs=[hbm, hbm, smem, smem, hbm, hbm],
        out_specs=(vmem, vmem, vmem),
        scratch_shapes=[
            pltpu.VMEM((2, stations, sources), bf16),
            pltpu.VMEM((1, sources), f32),
            pltpu.VMEM((2, own, stations), f32),
            pltpu.VMEM((2, own, n_dir), f32),
            pltpu.VMEM((2 * stations, sources), bf16),
            pltpu.VMEM((n_dir, 2, own, stations), bf16),
            pltpu.VMEM((n_dir, 2, own, stations), bf16),
            pltpu.VMEM((n_dir, 2, own, stations), f32),
            pltpu.VMEM((n_dir, 2, own, stations), f32),
            pltpu.VMEM((SLABS, 2 * PART // GROUP, GROUP, width), f32),
            pltpu.VMEM((2 * PART, own, 128), f32),
            pltpu.VMEM((n_dir, 3, own, 128), f32),
            pltpu.VMEM((SWEEPS + 1, own, 128), bf16),
            pltpu.VMEM((SWEEPS + 1, SLABS, per_slab, own, 128), bf16),
            pltpu.VMEM((SWEEPS, own, 128), bf16),
            pltpu.VMEM((SWEEPS, n_band, own, 128), bf16),
            pltpu.SemaphoreType.DMA((4,)),
            pltpu.SemaphoreType.DMA,
            pltpu.SemaphoreType.DMA((n_dir,)),
            pltpu.SemaphoreType.DMA((SWEEPS + 1,)),
            pltpu.SemaphoreType.DMA((SWEEPS + 1, SLABS)),
            pltpu.SemaphoreType.DMA((SWEEPS,)),
            pltpu.SemaphoreType.DMA((SWEEPS,)),
        ],
        compiler_params=pltpu.CompilerParams(
            collective_id=0, has_side_effects=True, vmem_limit_bytes=40 * 1024 * 1024
        ),
    )(
        *[pltpu.with_memory_space_constraint(value, pltpu.HBM) for value in (responses, fluxes)],
        counts,
        pltpu.with_memory_space_constraint(penalty, pltpu.HBM),
        pltpu.with_memory_space_constraint(visibilities, pltpu.HBM),
        pltpu.with_memory_space_constraint(jnp.transpose(start_gains, (0, 1, 3, 2)), pltpu.HBM),
    )
    return jnp.transpose(gains, (0, 1, 3, 2)), jnp.transpose(coefficients, (0, 1, 3, 2)), residual


def solution(mesh):
    in_specs = (
        P("band", "dir", None, None, None),
        P("band", "dir", None),
        P("dir"),
        P(),
        P("band", None, "dir", None),
        P("band", None, None, "dir"),
    )
    out_specs = (
        P("band", None, None, "dir"),
        P(None, None, None, "dir"),
        P("band", None, "dir", None),
    )
    return jax.shard_map(
        functools.partial(on_device, mesh.shape["band"], mesh.shape["dir"]),
        mesh=mesh,
        in_specs=in_specs,
        out_specs=out_specs,
        check_vma=False,
    )
```

time: 82.1 us -> 70 us (0.85)
  Pallas kernels: 73.7 us -> 66.7 us
  local copies, waits for them, and re-layouts: 6.88 us -> 1.86 us
    pallas_call x1, Pallas kernels: 73.7 us -> 66.7 us  [on_device(): pl.pallas_call(functools.partial(calibrate, n_band, n_dir), out_shape=(ja...]
    unnamed x10 -> x3, local copies, waits for them, and re-layouts: 5.5 us -> 1.86 us
    pallas_call x2 -> x0, local copies, waits for them, and re-layouts: 1.38 us -> none  [on_device(): pl.pallas_call(functools.partial(calibrate, n_band, n_dir), out_shape=(ja...]
where the time goes in v2:
time: 70 us; the launch traced here: 69.8 us
  Pallas kernels  66.7 us (95%)
  local copies, waits for them, and re-layouts  1.86 us (3%)
  between operations  1.29 us (2%)
    pallas_call x1, Pallas kernels, on_device(): pl.pallas_call(functools.partial(calibrate, n_band, n_dir), out_shape=(ja...  66.7 us
    unnamed x3, local copies, waits for them, and re-layouts  1.86 us

profile of v2, /device:TPU:1, one launch (start us, length us, event | category | flops | bytes accessed | tf_op | source)
XLA Modules:
  0.0 69.8 jit_solution(12901880660139657164)
XLA Ops:
  1.3 66.7 %shard_map.85 = (f32[1,2,16,32]{3,2,1,0:T(8,128)S(1)}, f32[3,2,16,32]{3,2,1,0:T(8,128)S(1)}, f32[1,2,16,512]{3,2,1,0:T(8,128)S(1)}) custom-call(bf16[1,1,2,512,1536]{4,3,2,1,0:T(8,128)(2,1)} %resp_hbm.1, f32[1,1,1536]{2,1,0:T(1,128)} %flux_hbm.1, s32[1]{0:T(128)S(6)} %copy.12.count_ref, f32[32]{0:T(128)} %penalty_ref.1, f32[1,2,16,512]{3,2,1,0:T(8,128)} %vis_hbm.1, ...), custom_call_target="tpu_custom_call" | custom-call | tf_op jit(solution)/shard_map/pallas_call | solution.py:403
  68.0 0.6 copy.13
  68.6 0.6 copy.14
  69.2 0.6 copy.15

commit v3 on v2

--- a/solution.py
+++ b/solution.py
@@ -71,6 +71,7 @@
     coh_recv,
     gain_send,
     gain_recv,
+    start_recv,
     mixed_send,
     mixed_recv,
 ):
@@ -90,11 +91,16 @@
             (
                 (start_hbm.at[0], start),
                 (flux_hbm.at[0], flux),
-                (resp_hbm.at[0, 0], resp),
                 (vis_hbm.at[0], vis),
             )
         )
     ]
+    slabs = [lax.rem(my_slab + offset, SLABS) for offset in (2, 1, 3, 0)]
+    for index, slab in enumerate(slabs):
+        rows = pl.ds(pl.multiple_of(slab * width, width), width)
+        loads.append(
+            pltpu.make_async_copy(resp_hbm.at[0, 0, :, rows], resp.at[:, rows], load_sem.at[3 + index])
+        )
     for load in loads:
         load.start()
 
@@ -163,10 +169,47 @@
                 device_id_type=MESH,
             ).start()
 
+    def send_start():
+        gain_out[0] = split(gains)
+        gain_in[0, my_slab, my_place] = gain_out[0]
+        for offset in (2, 1, 3):
+            pltpu.make_async_remote_copy(
+                src_ref=gain_out.at[0],
+                dst_ref=gain_in.at[0, my_slab, my_place],
+                send_sem=gain_send.at[0],
+                recv_sem=start_recv,
+                device_id=(band, lax.rem(my_slab + offset, SLABS) * per_slab + my_place),
+                device_id_type=MESH,
+            ).start()
+
+    def forward_start():
+        whole = gain_in.at[0, pl.ds(0, SLABS - 1), 0]
+        pltpu.make_async_copy(whole, whole, start_recv).wait()
+        for place in places:
+            if place is not my_place:
+                pltpu.make_async_remote_copy(
+                    src_ref=gain_in.at[0, :, my_place],
+                    dst_ref=gain_in.at[0, :, my_place],
+                    send_sem=gain_send.at[0],
+                    recv_sem=gain_recv.at[0, 0],
+                    device_id=(band, my_slab * per_slab + place),
+                    device_id_type=MESH,
+                ).start()
+
+    def receive_start():
+        whole = gain_in.at[0, :, pl.ds(0, per_slab - 1)]
+        pltpu.make_async_copy(whole, whole, gain_recv.at[0, 0]).wait()
+        for order in range(tiles):
+            unpack_tile(0, order)
+
     def receive_tile(slot, order):
         slab = near[order]
         whole = gain_in.at[slot, slab, pl.ds(0, per_slab - 1 if order == 0 else per_slab)]
         pltpu.make_async_copy(whole, whole, gain_recv.at[slot, slab]).wait()
+        unpack_tile(slot, order)
+
+    def unpack_tile(slot, order):
+        slab = near[order]
         packed = gain_in[slot, slab].reshape(width, 128)
         value = lax.dot_general(fold, packed, NT, preferred_element_type=jnp.float32)
         columns[order] = value.reshape(columns.shape[1:])
@@ -207,41 +250,21 @@
     loads[1].wait()
     live = lax.broadcasted_iota(jnp.int32, (1, sources), 1) < count_ref[0]
     weight = jnp.where(live, flux[...], 0.0)
-    loads[2].wait()
-    chunk = 64
-
-    def scale(step, carry):
-        for part in range(2):
-            begin = pl.multiple_of(step * chunk, chunk)
-            block = resp[part, pl.ds(begin, chunk), :].astype(jnp.float32)
-            scaled[pl.ds(pl.multiple_of(part * stations + begin, chunk), chunk), :] = (
-                block * weight
-            ).astype(jnp.bfloat16)
-        return carry
-
-    lax.fori_loop(0, stations // chunk, scale, 0)
-
-    def slab_step(step, carry):
-        slab = lax.rem(my_slab + 2 + 3 * step + 3 * (step // 2) + 2 * (step // 3), SLABS)
-        begin = pl.multiple_of(slab * width, width)
-        left = jnp.concatenate([resp[0, pl.ds(begin, width), :], resp[1, pl.ds(begin, width), :]], axis=0)
-        by_re = lax.dot_general(left, scaled[:stations], NT, preferred_element_type=jnp.float32)
-        by_im = lax.dot_general(left, scaled[stations:], NT, preferred_element_type=jnp.float32)
+
+    def combine(by_re, by_im, begin_row, begin_col):
+        count = by_re.shape[1]
         real = by_re[:width] + by_im[width:]
         imag = by_re[width:] - by_im[:width]
-        off = (lax.broadcasted_iota(jnp.int32, (width, stations), 0) + begin) != (
-            lax.broadcasted_iota(jnp.int32, (width, stations), 1)
+        off = (lax.broadcasted_iota(jnp.int32, (width, count), 0) + begin_row) != (
+            lax.broadcasted_iota(jnp.int32, (width, count), 1) + begin_col
         )
-        shape = (per_slab, own, stations)
-        first_dir = slab * per_slab
-        coh_out[pl.ds(first_dir, per_slab), 0] = jnp.where(off, real, 0.0).astype(jnp.bfloat16).reshape(shape)
-        coh_out[pl.ds(first_dir, per_slab), 1] = jnp.where(off, imag, 0.0).astype(jnp.bfloat16).reshape(shape)
-
-        @pl.when(step == 0)
-        def _():
-            pl.semaphore_wait(barrier, n_dir + n_band - 2)
-            send_gains(0, gains)
-
+        shape = (per_slab, own, count)
+        return [jnp.where(off, value, 0.0).astype(jnp.bfloat16).reshape(shape) for value in (real, imag)]
+
+    def left_rows(begin):
+        return jnp.concatenate([resp[0, pl.ds(begin, width), :], resp[1, pl.ds(begin, width), :]], axis=0)
+
+    def send_rows(first_dir):
         def send(place, inner):
             peer = first_dir + lax.rem(my_place + per_slab // 2 + place, per_slab)
 
@@ -259,16 +282,49 @@
             return inner
 
         lax.fori_loop(0, per_slab, send, 0)
+
+    far_begin = pl.multiple_of(slabs[0] * width, width)
+    far_dirs = pl.ds(slabs[0] * per_slab, per_slab)
+    for index, slab in enumerate(slabs):
+        loads[3 + index].wait()
+        begin = pl.multiple_of(slab * width, width)
+        here = pl.ds(begin, width)
+        pieces = []
+        for part in range(2):
+            piece = (resp[part, here, :].astype(jnp.float32) * weight).astype(jnp.bfloat16)
+            scaled[pl.ds(pl.multiple_of(part * stations + begin, width), width), :] = piece
+            pieces.append(piece)
+        right = jnp.concatenate(pieces, axis=0)
+        product = lax.dot_general(left_rows(far_begin), right, NT, preferred_element_type=jnp.float32)
+        real, imag = combine(product[:, :width], product[:, width:], far_begin, begin)
+        coh_out[far_dirs, 0, :, here] = real
+        coh_out[far_dirs, 1, :, here] = imag
+    pl.semaphore_wait(barrier, n_dir + n_band - 2)
+    send_start()
+    send_rows(slabs[0] * per_slab)
+
+    def slab_step(step, carry):
+        slab = lax.rem(my_slab + 2 + 3 * step + 3 * (step // 2) + 2 * (step // 3), SLABS)
+        begin = pl.multiple_of(slab * width, width)
+        left = left_rows(begin)
+        by_re = lax.dot_general(left, scaled[:stations], NT, preferred_element_type=jnp.float32)
+        by_im = lax.dot_general(left, scaled[stations:], NT, preferred_element_type=jnp.float32)
+        first_dir = slab * per_slab
+        real, imag = combine(by_re, by_im, begin, 0)
+        coh_out[pl.ds(first_dir, per_slab), 0] = real
+        coh_out[pl.ds(first_dir, per_slab), 1] = imag
+        send_rows(first_dir)
         return carry
 
-    lax.fori_loop(0, SLABS, slab_step, 0)
+    lax.fori_loop(1, SLABS, slab_step, 0)
     coh_in[me] = coh_out[me]
     widen(gains)
-    loads[3].wait()
+    loads[2].wait()
     row_id = lax.broadcasted_iota(jnp.int32, (own, stations), 0) + me * own
     col_id = lax.broadcasted_iota(jnp.int32, (own, stations), 1)
     for part in range(2):
         vis[part] = jnp.where(row_id == col_id, 0.0, vis[part])
+    forward_start()
 
     def advance(index, group, member, order, totals):
         here = pl.ds(order * width, width)
@@ -291,7 +347,10 @@
         return vis[0, :, spans[order]] - totals[0], vis[1, :, spans[order]] - totals[1]
 
     def project_first():
-        def step(group, totals):
+        groups = n_dir // GROUP
+
+        def step(turn, totals):
+            group = lax.rem(me // GROUP + turn + turn // 2 - 2 * (turn // 3), groups)
             for member in range(GROUP):
                 index = group * GROUP + member
 
@@ -348,15 +407,21 @@
 
         return lax.fori_loop(0, n_dir, step, (zero, zero), unroll=GROUP)
 
+    def agree(slot, value, duals):
+        coefficients = receive_mixed(slot)
+        target = coefficients[0] + own_place * coefficients[1] + own_place * own_place * coefficients[2]
+        return target, duals + value - target
+
     target = gains
     duals = zero
     for sweep in range(SWEEPS):
         if sweep == 0:
-            for order in range(tiles):
-                receive_tile(0, order)
+            receive_start()
             numer, weights = reduce(range(tiles), project_first(), True, True)
         else:
             for order in range(tiles):
+                if order == tiles - 1:
+                    target, duals = agree(sweep - 1, gains, duals)
                 receive_tile(sweep, order)
                 residual = project_tile(order)
                 numer, weights = reduce([order], [residual], order == 0, order == tiles - 1)
@@ -368,13 +433,12 @@
         if sweep == SWEEPS - 1:
             for part in range(2):
                 gains_ref[0, part] = gains[:, part * PART : part * PART + n_dir]
-        coefficients = receive_mixed(sweep)
-        target = coefficients[0] + own_place * coefficients[1] + own_place * own_place * coefficients[2]
-        duals = duals + gains - target
-    for order in range(3):
-        for part in range(2):
-            coeff_ref[order, part] = coefficients[order][:, part * PART : part * PART + n_dir]
     for order in range(tiles):
+        if order == tiles - 1:
+            coefficients = receive_mixed(SWEEPS - 1)
+            for index in range(3):
+                for part in range(2):
+                    coeff_ref[index, part] = coefficients[index][:, part * PART : part * PART + n_dir]
         receive_tile(SWEEPS, order)
         residual = project_tile(order)
         for part in range(2):
@@ -426,11 +490,12 @@
             pltpu.VMEM((SWEEPS + 1, SLABS, per_slab, own, 128), bf16),
             pltpu.VMEM((SWEEPS, own, 128), bf16),
             pltpu.VMEM((SWEEPS, n_band, own, 128), bf16),
-            pltpu.SemaphoreType.DMA((4,)),
+            pltpu.SemaphoreType.DMA((3 + SLABS,)),
             pltpu.SemaphoreType.DMA,
             pltpu.SemaphoreType.DMA((n_dir,)),
             pltpu.SemaphoreType.DMA((SWEEPS + 1,)),
             pltpu.SemaphoreType.DMA((SWEEPS + 1, SLABS)),
+            pltpu.SemaphoreType.DMA,
             pltpu.SemaphoreType.DMA((SWEEPS,)),
             pltpu.SemaphoreType.DMA((SWEEPS,)),
         ],

time: 70 us -> 67 us (0.957)
  Pallas kernels: 66.7 us -> 63.7 us
    pallas_call x1, Pallas kernels: 66.7 us -> 63.7 us  [on_device(): pl.pallas_call(functools.partial(calibrate, n_band, n_dir), out_shape=(ja...]
where the time goes in v3:
time: 67 us; the launch traced here: 66.8 us
  Pallas kernels  63.7 us (95%)
  local copies, waits for them, and re-layouts  1.86 us (3%)
  between operations  1.29 us (2%)
    pallas_call x1, Pallas kernels, on_device(): pl.pallas_call(functools.partial(calibrate, n_band, n_dir), out_shape=(ja...  63.7 us
    unnamed x3, local copies, waits for them, and re-layouts  1.86 us

profile of v3, /device:TPU:1, one launch (start us, length us, event | category | flops | bytes accessed | tf_op | source)
XLA Modules:
  0.0 66.8 jit_solution(9164909045531573985)
XLA Ops:
  1.3 63.7 %shard_map.85 = (f32[1,2,16,32]{3,2,1,0:T(8,128)S(1)}, f32[3,2,16,32]{3,2,1,0:T(8,128)S(1)}, f32[1,2,16,512]{3,2,1,0:T(8,128)S(1)}) custom-call(bf16[1,1,2,512,1536]{4,3,2,1,0:T(8,128)(2,1)} %resp_hbm.1, f32[1,1,1536]{2,1,0:T(1,128)} %flux_hbm.1, s32[1]{0:T(128)S(6)} %copy.12.count_ref, f32[32]{0:T(128)} %penalty_ref.1, f32[1,2,16,512]{3,2,1,0:T(8,128)} %vis_hbm.1, ...), custom_call_target="tpu_custom_call" | custom-call | tf_op jit(solution)/shard_map/pallas_call | solution.py:467
  65.0 0.6 copy.13
  65.6 0.6 copy.14
  66.2 0.6 copy.15

commit v4 on v3

--- a/solution.py
+++ b/solution.py
@@ -43,8 +43,8 @@
     n_dir,
     resp_hbm,
     flux_hbm,
-    count_ref,
-    penalty_ref,
+    count_hbm,
+    penalty_hbm,
     vis_hbm,
     start_hbm,
     gains_ref,
@@ -54,6 +54,8 @@
     flux,
     vis,
     start,
+    count,
+    penalty,
     scaled,
     coh_out,
     coh_in,
@@ -85,23 +87,25 @@
     my_slab = me // per_slab
     my_place = lax.rem(me, per_slab)
 
-    loads = [
-        pltpu.make_async_copy(source, goal, load_sem.at[index])
+    slabs = [lax.rem(my_slab + offset, SLABS) for offset in (2, 1, 3, 0)]
+    chunks = [pl.ds(pl.multiple_of(slab * width, width), width) for slab in slabs]
+    small = [
+        pltpu.make_async_copy(source, goal, load_sem.at[SLABS + index])
         for index, (source, goal) in enumerate(
             (
+                (flux_hbm.at[0], flux),
+                (count_hbm, count),
                 (start_hbm.at[0], start),
-                (flux_hbm.at[0], flux),
+                (penalty_hbm, penalty),
                 (vis_hbm.at[0], vis),
             )
         )
     ]
-    slabs = [lax.rem(my_slab + offset, SLABS) for offset in (2, 1, 3, 0)]
-    for index, slab in enumerate(slabs):
-        rows = pl.ds(pl.multiple_of(slab * width, width), width)
-        loads.append(
-            pltpu.make_async_copy(resp_hbm.at[0, 0, :, rows], resp.at[:, rows], load_sem.at[3 + index])
-        )
-    for load in loads:
+    large = [
+        pltpu.make_async_copy(resp_hbm.at[0, 0, :, rows], resp.at[:, rows], load_sem.at[index])
+        for index, rows in enumerate(chunks)
+    ]
+    for load in small[:2] + large + small[2:]:
         load.start()
 
     barrier = pltpu.get_barrier_semaphore()
@@ -134,18 +138,6 @@
         high = value.astype(jnp.bfloat16).astype(jnp.float32)
         return jnp.where(low_half, high, value - high).astype(jnp.bfloat16)
 
-    strength = jnp.ones((own, 128), jnp.float32)
-    for index in range(n_dir):
-        strength = jnp.where(dir_lane == index, penalty_ref[index], strength)
-
-    loads[0].wait()
-    pieces = []
-    for part in range(2):
-        pieces.append(start[part])
-        if n_dir < PART:
-            pieces.append(jnp.zeros((own, PART - n_dir), jnp.float32))
-    gains = jnp.concatenate(pieces + pieces, axis=1)
-
     near = [lax.rem(my_slab + offset, SLABS) for offset in (0, 1, 3, 2)]
     spans = [pl.ds(pl.multiple_of(slab * width, width), width) for slab in near]
 
@@ -169,7 +161,7 @@
                 device_id_type=MESH,
             ).start()
 
-    def send_start():
+    def send_start(gains):
         gain_out[0] = split(gains)
         gain_in[0, my_slab, my_place] = gain_out[0]
         for offset in (2, 1, 3):
@@ -247,8 +239,9 @@
             for row in range(3)
         ]
 
-    loads[1].wait()
-    live = lax.broadcasted_iota(jnp.int32, (1, sources), 1) < count_ref[0]
+    small[0].wait()
+    small[1].wait()
+    live = lax.broadcasted_iota(jnp.int32, (1, sources), 1) < count[0]
     weight = jnp.where(live, flux[...], 0.0)
 
     def combine(by_re, by_im, begin_row, begin_col):
@@ -286,7 +279,7 @@
     far_begin = pl.multiple_of(slabs[0] * width, width)
     far_dirs = pl.ds(slabs[0] * per_slab, per_slab)
     for index, slab in enumerate(slabs):
-        loads[3 + index].wait()
+        large[index].wait()
         begin = pl.multiple_of(slab * width, width)
         here = pl.ds(begin, width)
         pieces = []
@@ -300,7 +293,20 @@
         coh_out[far_dirs, 0, :, here] = real
         coh_out[far_dirs, 1, :, here] = imag
     pl.semaphore_wait(barrier, n_dir + n_band - 2)
-    send_start()
+    small[3].wait()
+    strength = jnp.ones((own, 128), jnp.float32)
+    for index in range(n_dir):
+        strength = jnp.where(dir_lane == index, penalty[index], strength)
+
+    small[2].wait()
+    pieces = []
+    for part in range(2):
+        pieces.append(start[part])
+        if n_dir < PART:
+            pieces.append(jnp.zeros((own, PART - n_dir), jnp.float32))
+    gains = jnp.concatenate(pieces + pieces, axis=1)
+
+    send_start(gains)
     send_rows(slabs[0] * per_slab)
 
     def slab_step(step, carry):
@@ -319,7 +325,7 @@
     lax.fori_loop(1, SLABS, slab_step, 0)
     coh_in[me] = coh_out[me]
     widen(gains)
-    loads[2].wait()
+    small[4].wait()
     row_id = lax.broadcasted_iota(jnp.int32, (own, stations), 0) + me * own
     col_id = lax.broadcasted_iota(jnp.int32, (own, stations), 1)
     for part in range(2):
@@ -405,7 +411,7 @@
             weights = jnp.where(dir_lane == index, sum_weight, weights)
             return numer, weights
 
-        return lax.fori_loop(0, n_dir, step, (zero, zero), unroll=GROUP)
+        return lax.fori_loop(0, n_dir, step, (zero, zero), unroll=n_dir if closing else GROUP)
 
     def agree(slot, value, duals):
         coefficients = receive_mixed(slot)
@@ -462,7 +468,6 @@
     per_slab = n_dir // SLABS
     hbm = pl.BlockSpec(memory_space=pltpu.HBM)
     vmem = pl.BlockSpec(memory_space=pltpu.VMEM)
-    smem = pl.BlockSpec(memory_space=pltpu.SMEM)
     bf16, f32 = jnp.bfloat16, jnp.float32
     gains, coefficients, residual = pl.pallas_call(
         functools.partial(calibrate, n_band, n_dir),
@@ -471,13 +476,15 @@
             jax.ShapeDtypeStruct((3, 2, own, n_dir), f32),
             jax.ShapeDtypeStruct((1, 2, own, stations), f32),
         ),
-        in_specs=[hbm, hbm, smem, smem, hbm, hbm],
+        in_specs=[hbm] * 6,
         out_specs=(vmem, vmem, vmem),
         scratch_shapes=[
             pltpu.VMEM((2, stations, sources), bf16),
             pltpu.VMEM((1, sources), f32),
             pltpu.VMEM((2, own, stations), f32),
             pltpu.VMEM((2, own, n_dir), f32),
+            pltpu.SMEM((1,), jnp.int32),
+            pltpu.SMEM((n_dir,), f32),
             pltpu.VMEM((2 * stations, sources), bf16),
             pltpu.VMEM((n_dir, 2, own, stations), bf16),
             pltpu.VMEM((n_dir, 2, own, stations), bf16),
@@ -490,7 +497,7 @@
             pltpu.VMEM((SWEEPS + 1, SLABS, per_slab, own, 128), bf16),
             pltpu.VMEM((SWEEPS, own, 128), bf16),
             pltpu.VMEM((SWEEPS, n_band, own, 128), bf16),
-            pltpu.SemaphoreType.DMA((3 + SLABS,)),
+            pltpu.SemaphoreType.DMA((SLABS + 5,)),
             pltpu.SemaphoreType.DMA,
             pltpu.SemaphoreType.DMA((n_dir,)),
             pltpu.SemaphoreType.DMA((SWEEPS + 1,)),

time: 67 us -> 65.7 us (0.981)
  Pallas kernels: 63.7 us -> 62.4 us
    pallas_call x1, Pallas kernels: 63.7 us -> 62.4 us  [on_device(): pl.pallas_call(functools.partial(calibrate, n_band, n_dir), out_shape=(ja...]
where the time goes in v4:
time: 65.7 us; the launch traced here: 65.6 us
  Pallas kernels  62.4 us (95%)
  local copies, waits for them, and re-layouts  1.86 us (3%)
  between operations  1.29 us (2%)
    pallas_call x1, Pallas kernels, on_device(): pl.pallas_call(functools.partial(calibrate, n_band, n_dir), out_shape=(ja...  62.4 us
    unnamed x3, local copies, waits for them, and re-layouts  1.86 us

profile of v4, /device:TPU:1, one launch (start us, length us, event | category | flops | bytes accessed | tf_op | source)
XLA Modules:
  0.0 65.6 jit_solution(7655485775053725993)
XLA Ops:
  1.3 62.4 %shard_map.85 = (f32[1,2,16,32]{3,2,1,0:T(8,128)S(1)}, f32[3,2,16,32]{3,2,1,0:T(8,128)S(1)}, f32[1,2,16,512]{3,2,1,0:T(8,128)S(1)}) custom-call(bf16[1,1,2,512,1536]{4,3,2,1,0:T(8,128)(2,1)} %resp_hbm.1, f32[1,1,1536]{2,1,0:T(1,128)} %flux_hbm.1, s32[1]{0:T(128)S(6)} %copy.12.count_hbm, f32[32]{0:T(128)} %penalty_hbm.1, f32[1,2,16,512]{3,2,1,0:T(8,128)} %vis_hbm.1, ...), custom_call_target="tpu_custom_call" | custom-call | tf_op jit(solution)/shard_map/pallas_call | solution.py:472
  63.7 0.6 copy.13
  64.3 0.6 copy.14
  64.9 0.6 copy.15

commit v5 on v4

--- a/solution.py
+++ b/solution.py
@@ -459,6 +459,11 @@
     for slot in range(SWEEPS):
         whole = mixed_in.at[slot, pl.ds(0, n_band - 1)]
         pltpu.make_async_copy(whole, whole, mixed_send.at[slot]).wait()
+
+
+def hand_over(*refs):
+    for source, goal in zip(refs[:3], refs[3:]):
+        goal[...] = source[...]
 
 
 def on_device(n_band, n_dir, responses, fluxes, counts, penalty, visibilities, start_gains):
@@ -516,6 +521,14 @@
         pltpu.with_memory_space_constraint(visibilities, pltpu.HBM),
         pltpu.with_memory_space_constraint(jnp.transpose(start_gains, (0, 1, 3, 2)), pltpu.HBM),
     )
+    results = (gains, coefficients, residual)
+    gains, coefficients, residual = pl.pallas_call(
+        hand_over,
+        out_shape=tuple(jax.ShapeDtypeStruct(value.shape, value.dtype) for value in results),
+        in_specs=[vmem] * 3,
+        out_specs=(vmem,) * 3,
+        compiler_params=pltpu.CompilerParams(vmem_limit_bytes=4 * 1024 * 1024),
+    )(*results)
     return jnp.transpose(gains, (0, 1, 3, 2)), jnp.transpose(coefficients, (0, 1, 3, 2)), residual
 
 

time: 65.7 us -> 64.5 us (0.982)
  local copies, waits for them, and re-layouts: 1.86 us -> 0 us
  Pallas kernels: 62.4 us -> 63.1 us
    unnamed x3 -> x0, local copies, waits for them, and re-layouts: 1.86 us -> none
    pallas_call x0 -> x1, Pallas kernels: none -> 0.66 us  [on_device(): pl.pallas_call(hand_over, out_shape=tuple((jax.ShapeDtypeStruct(value.sha...]
where the time goes in v5:
time: 64.5 us; the launch traced here: 64.4 us
  Pallas kernels  63.1 us (98%)
  between operations  1.28 us (2%)
    pallas_call x1, Pallas kernels, on_device(): pl.pallas_call(functools.partial(calibrate, n_band, n_dir), out_shape=(ja...  62.4 us

profile of v5, /device:TPU:1, one launch (start us, length us, event | category | flops | bytes accessed | tf_op | source)
XLA Modules:
  0.0 64.4 jit_solution(9288765553969391343)
XLA Ops:
  1.3 62.4 %shard_map.85 = (f32[1,2,16,32]{3,2,1,0:T(8,128)S(1)}, f32[3,2,16,32]{3,2,1,0:T(8,128)S(1)}, f32[1,2,16,512]{3,2,1,0:T(8,128)S(1)}) custom-call(bf16[1,1,2,512,1536]{4,3,2,1,0:T(8,128)(2,1)} %resp_hbm.1, f32[1,1,1536]{2,1,0:T(1,128)} %flux_hbm.1, s32[1]{0:T(128)S(6)} %copy.9.count_hbm, f32[32]{0:T(128)} %penalty_hbm.1, f32[1,2,16,512]{3,2,1,0:T(8,128)} %vis_hbm.1, ...), custom_call_target="tpu_custom_call" | custom-call | tf_op jit(solution)/shard_map/pallas_call | solution.py:477
  63.7 0.7 %shard_map.86 = (f32[1,2,16,32]{3,2,1,0:T(8,128)}, f32[3,2,16,32]{3,2,1,0:T(8,128)}, f32[1,2,16,512]{3,2,1,0:T(8,128)}) custom-call(f32[1,2,16,32]{3,2,1,0:T(8,128)S(1)} %get-tuple-element.9.refs_0_, f32[3,2,16,32]{3,2,1,0:T(8,128)S(1)} %get-tuple-element.10.refs_1_, f32[1,2,16,512]{3,2,1,0:T(8,128)S(1)} %get-tuple-element.11.refs_2_), custom_call_target="tpu_custom_call" | custom-call | tf_op jit(solution)/shard_map/pallas_call | solution.py:525

commit v6 on v5

--- a/solution.py
+++ b/solution.py
@@ -105,7 +105,7 @@
         pltpu.make_async_copy(resp_hbm.at[0, 0, :, rows], resp.at[:, rows], load_sem.at[index])
         for index, rows in enumerate(chunks)
     ]
-    for load in small[:2] + large + small[2:]:
+    for load in small[:1] + large:
         load.start()
 
     barrier = pltpu.get_barrier_semaphore()
@@ -123,6 +123,8 @@
         pl.semaphore_signal(barrier, inc=1, device_id=(band, peer), device_id_type=MESH)
     for peer in bands:
         pl.semaphore_signal(barrier, inc=1, device_id=(peer, me), device_id_type=MESH)
+    for load in small[1:]:
+        load.start()
 
     lane = lax.broadcasted_iota(jnp.int32, (own, 128), 1)
     dir_lane = lane % PART
@@ -332,7 +334,7 @@
         vis[part] = jnp.where(row_id == col_id, 0.0, vis[part])
     forward_start()
 
-    def advance(index, group, member, order, totals):
+    def advance(index, group, member, order, totals, keep=True):
         here = pl.ds(order * width, width)
         coh_re = coh[index, 0, :, here]
         coh_im = coh[index, 1, :, here]
@@ -342,8 +344,9 @@
         row_im = rows_wide[PART + index]
         along_re = coh_re * col_re + coh_im * col_im
         along_im = coh_im * col_re - coh_re * col_im
-        along[index, 0, :, here] = along_re
-        along[index, 1, :, here] = along_im
+        if keep:
+            along[index, 0, :, here] = along_re
+            along[index, 1, :, here] = along_im
         return (
             totals[0] + (row_re * along_re - row_im * along_im),
             totals[1] + (row_re * along_im + row_im * along_re),
@@ -377,10 +380,10 @@
         totals = lax.fori_loop(0, n_dir // GROUP, step, ((zero, zero),) * tiles)
         return [left_over(order, totals[order]) for order in range(tiles)]
 
-    def project_tile(order):
+    def project_tile(order, keep=True):
         def step(group, totals):
             for member in range(GROUP):
-                totals = advance(group * GROUP + member, group, member, order, totals)
+                totals = advance(group * GROUP + member, group, member, order, totals, keep)
             return totals
 
         return left_over(order, lax.fori_loop(0, n_dir // GROUP, step, (zero, zero)))
@@ -446,7 +449,7 @@
                 for part in range(2):
                     coeff_ref[index, part] = coefficients[index][:, part * PART : part * PART + n_dir]
         receive_tile(SWEEPS, order)
-        residual = project_tile(order)
+        residual = project_tile(order, keep=False)
         for part in range(2):
             resid_ref[0, part, :, spans[order]] = residual[part]
 

time: 64.5 us -> 64.5 us (level)
  no operation moved by 1% of the time
where the time goes in v6:
time: 64.5 us; the launch traced here: 64.4 us
  Pallas kernels  63.1 us (98%)
  between operations  1.28 us (2%)
    pallas_call x1, Pallas kernels, on_device(): pl.pallas_call(functools.partial(calibrate, n_band, n_dir), out_shape=(ja...  62.4 us

profile of v6, /device:TPU:1, one launch (start us, length us, event | category | flops | bytes accessed | tf_op | source)
XLA Modules:
  0.0 64.4 jit_solution(6185139272435630245)
XLA Ops:
  1.3 62.4 %shard_map.85 = (f32[1,2,16,32]{3,2,1,0:T(8,128)S(1)}, f32[3,2,16,32]{3,2,1,0:T(8,128)S(1)}, f32[1,2,16,512]{3,2,1,0:T(8,128)S(1)}) custom-call(bf16[1,1,2,512,1536]{4,3,2,1,0:T(8,128)(2,1)} %resp_hbm.1, f32[1,1,1536]{2,1,0:T(1,128)} %flux_hbm.1, s32[1]{0:T(128)S(6)} %copy.9.count_hbm, f32[32]{0:T(128)} %penalty_hbm.1, f32[1,2,16,512]{3,2,1,0:T(8,128)} %vis_hbm.1, ...), custom_call_target="tpu_custom_call" | custom-call | tf_op jit(solution)/shard_map/pallas_call | solution.py:480
  63.7 0.7 %shard_map.86 = (f32[1,2,16,32]{3,2,1,0:T(8,128)}, f32[3,2,16,32]{3,2,1,0:T(8,128)}, f32[1,2,16,512]{3,2,1,0:T(8,128)}) custom-call(f32[1,2,16,32]{3,2,1,0:T(8,128)S(1)} %get-tuple-element.9.refs_0_, f32[3,2,16,32]{3,2,1,0:T(8,128)S(1)} %get-tuple-element.10.refs_1_, f32[1,2,16,512]{3,2,1,0:T(8,128)S(1)} %get-tuple-element.11.refs_2_), custom_call_target="tpu_custom_call" | custom-call | tf_op jit(solution)/shard_map/pallas_call | solution.py:528
